TPU v7x, 128 devices: a whole 4x4x4 slice. The times are simulated.
128 devices in a mesh: pole: 4 (over y_lo, core), dom: 32 (over z, x, y_hi).
Axes of the slice: x: 4, y: 4 (y_hi: 2, y_lo: 2; y = y_hi * 2 + y_lo), z: 4, core: 2. Of those that a mesh axis runs over, the one named last changes fastest.
Arguments:
- initial_block: bfloat16 [32, 8, 512, 256], P('dom'), may hold values from -24 to 24
- coupling: bfloat16 [32, 8, 512, 512], P('dom'), may hold values from -0.125 to 0.125
- pivots: bfloat16 [4, 32, 8, 2, 512, 512], P('pole', 'dom'), may hold values from -0.125 to 0.125
- interface: bfloat16 [4, 32, 3, 2, 512, 512], P('pole', 'dom'), may hold values from -0.1875 to 0.1875
- pole_values: float32 [4, 4], P('pole'), may hold values from 0.5 to 1.5
Outputs:
- filtered_basis: float32 [32, 8, 512, 256], P('dom', 'pole')
- rayleigh: float32 [256, 256], replicated
All inputs are finite; a program needn't handle non-finite values.
Results may differ from a plain program's by a relative error of at most 0.008.
Values sent between devices are 32-bit elements; how exact they have to be, the bound alone decides.
A program may use at most 192 MiB of HBM per device.

v0:
```python
import jax
import jax.numpy as jnp
from jax import lax
from jax.sharding import PartitionSpec as P

B = 512
M = 256


def shifted(x, axis, by):
    length = lax.axis_size(axis)
    pairs = [(i, i + by) for i in range(length) if 0 <= i + by < length]
    return lax.ppermute(x, axis, pairs)


def lower_solve(factor, right_side):
    return lax.linalg.triangular_solve(factor, right_side, left_side=True, lower=True)


def complex_product(matrix, vectors):
    block_order = matrix.shape[1]
    half_width = vectors.shape[1] // 2
    stacked = matrix.reshape(2 * block_order, block_order)
    stacked_out = jnp.dot(stacked, vectors.astype(jnp.bfloat16), preferred_element_type=jnp.float32)
    real_part = stacked_out[:block_order, :half_width] - stacked_out[block_order:, half_width:]
    imag_part = stacked_out[:block_order, half_width:] + stacked_out[block_order:, :half_width]
    return jnp.concatenate([real_part, imag_part], axis=1)


def real_product(matrix, vectors):
    return jnp.dot(matrix, vectors.astype(jnp.bfloat16), preferred_element_type=jnp.float32)


def transposed_product(matrix, vectors):
    return lax.dot_general(
        matrix,
        vectors.astype(jnp.bfloat16),
        (((0,), (0,)), ((), ())),
        preferred_element_type=jnp.float32,
    )


def inner_products(left, right_side):
    return lax.dot_general(
        left,
        right_side,
        (((0,), (0,)), ((), ())),
        precision=lax.Precision.HIGHEST,
        preferred_element_type=jnp.float32,
    )


def partition_solve(inverse, coupled, source):
    previous = jnp.roll(coupled, 1, axis=0)
    initial = jnp.zeros(source.shape[1:], jnp.float32)

    def forward_step(carried, members):
        block_inverse, given, couple_prev = members
        result = complex_product(block_inverse, given + transposed_product(couple_prev, carried))
        return (result, result)

    unused, forward = lax.scan(forward_step, initial, (inverse, source, previous))

    def backward_step(carried, members):
        block_inverse, partial_value, couple_next = members
        result = partial_value + complex_product(block_inverse, real_product(couple_next, carried))
        return (result, result)

    unused, backward = lax.scan(backward_step, initial, (inverse, forward, coupled), reverse=True)
    return backward


def on_device(initial_block, coupling, pivots, interface, pole_values):
    blocks = coupling.shape[1]
    coupled = coupling[0]
    inverse = pivots[0, 0]
    factors = interface[0, 0]
    real_start = initial_block[0].astype(jnp.float32)
    source = jnp.concatenate([real_start, jnp.zeros_like(real_start)], axis=-1)
    first = partition_solve(inverse, coupled, source)
    bottom = first[blocks - 1]
    top = first[0]
    top_next = shifted(top, "dom", -1)
    below = complex_product(factors[0], bottom) - complex_product(factors[1], top_next)
    topmost = lax.axis_index("dom") == lax.axis_size("dom") - 1
    above = jnp.where(
        topmost, jnp.zeros_like(top_next), top_next - complex_product(factors[2], below)
    )
    link = coupled[blocks - 1]
    lifted = transposed_product(link, below)
    arriving = shifted(lifted, "dom", 1)
    update = source.at[0].add(arriving)
    update = update.at[blocks - 1].add(real_product(link, above))
    second = partition_solve(inverse, coupled, update)
    real_z = pole_values[0, 0]
    imag_z = pole_values[0, 1]
    real_w = pole_values[0, 2]
    imag_w = pole_values[0, 3]
    real_x = second[..., :M]
    imag_x = second[..., M:]
    filtered_term = real_w * real_x - imag_w * imag_x
    shifted_term = (
        (real_w * real_z - imag_w * imag_z) * real_x
        - (real_w * imag_z + imag_w * real_z) * imag_x
        - real_w * real_start
    )
    count = blocks // lax.axis_size("pole")
    owned, shifted_owned = (
        lax.psum_scatter(filtered_term[None], "pole", scatter_dimension=1, tiled=True),
        lax.psum_scatter(shifted_term[None], "pole", scatter_dimension=1, tiled=True),
    )
    own_rows = owned[0].reshape(count * B, M)
    gram_part = inner_products(own_rows, own_rows)
    projected_part = inner_products(own_rows, shifted_owned[0].reshape(count * B, M))
    gram_total, projected_total = lax.psum((gram_part, projected_part), ("pole", "dom"))
    row_total = blocks * B * lax.axis_size("dom")
    gram = gram_total / row_total
    projected = projected_total / row_total
    factor = jnp.linalg.cholesky(gram)
    filtered_basis = lower_solve(factor, own_rows.T).T.reshape(1, count, B, M)
    middle = lower_solve(factor, projected)
    rayleigh = lower_solve(factor, middle.T).T
    return (filtered_basis, rayleigh)


def solution(mesh):
    in_specs = (
        P("dom", None, None, None),
        P("dom", None, None, None),
        P("pole", "dom", None, None, None, None),
        P("pole", "dom", None, None, None, None),
        P("pole", None),
    )
    out_specs = (P("dom", "pole", None, None), P())
    return jax.shard_map(
        on_device, mesh=mesh, in_specs=in_specs, out_specs=out_specs, check_vma=False
    )
```

profile of v0, /device:TPU:1, one launch (start us, length us, event | category | flops | bytes accessed | tf_op | source)
XLA Modules:
  0.0 714.1 jit_solution(7158494593496729926)
XLA Ops:
  7.2 4.2 slice_bitcast_fusion
  18.0 4.2 concatenate.76
  24.6 4.3 broadcast.158.clone.2
  29.7 65.3 %while.65 = (s32[]{:T(128)}, bf16[512,512]{0,1:T(8,128)(2,1)}, f32[8,512,512]{1,2,0:T(8,128)}, bf16[8,2,512,512]{3,2,1,0:T(8,128)(2,1)}, f32[8,512,512]{1,2,0:T(8,128)}, /*index=5*/bf16[8,512,512]{2,1,0:T(8,128)(2,1)}, s32[]{:T(128)}) while((s32[]{:T(128)}, bf16[512,512]{0,1:T(8,128)(2,1)}, f32[8,512,512]{1,2,0:T(8,128)}, ...), condition=%wide.region_1.2_spmd, body=%wide.region_0.1_spmd.sunk | while | flops 806617088 | bytes 17302612 | solution.py:62
  95.0 4.3 broadcast.158.clone.1
  99.3 67.7 %while.68 = (s32[]{:T(128)}, bf16[512,512]{0,1:T(8,128)(2,1)}, f32[8,512,512]{1,2,0:T(8,128)}, f32[8,512,512]{1,2,0:T(8,128)}, bf16[8,2,512,512]{3,2,1,0:T(8,128...) while((s32[]{:T(128)}, bf16[512,512]{0,1:T(8,128)(2,1)}, ...), condition=%wide.region_3.4_spmd.clone, body=%wide.region_2.3_spmd.clone.sunk | while | flops 807403520 | bytes 15204483 | solution.py:69
  173.9 22.7 %collective-permute-done = f32[512,512]{0,1:T(8,128)S(1)} collective-permute-done((f32[512,512]{0,1:T(8,128)S(1)}, f32[512,512]{0,1:T(8,128)S(1)}, u32[]{:S(2)}, u32[]{:S(2)}) %collective-permute-start) | collective-permute-done | bytes 1048608 | tf_op jit(solution)/shard_map/ppermute | solution.py:13
  200.3 7.2 %collective-permute-start.1 = (f32[512,512]{0,1:T(8,128)}, f32[512,512]{0,1:T(8,128)}, u32[]{:S(2)}, u32[]{:S(2)}) collective-permute-start(f32[512,512]{0,1:T(8,128)} %convolution_bitcast_fusion.4), channel_id=1, source_target_pairs={{0,1},{1,2},{2,3},{3,4},{4,5},{5,6},{6,7},{7,8},{8,9},{9,10},{10,1... | collective-permute-start | bytes 3145736 | tf_op jit(solution)/shard_map/ppermute | solution.py:13
  213.9 13.3 %collective-permute-done.1 = f32[512,512]{0,1:T(8,128)} collective-permute-done((f32[512,512]{0,1:T(8,128)}, f32[512,512]{0,1:T(8,128)}, u32[]{:S(2)}, u32[]{:S(2)}) %collective-permute-start.1) | collective-permute-done | bytes 1048608 | tf_op jit(solution)/shard_map/ppermute | solution.py:13
  232.4 4.3 broadcast.158.clone
  237.6 65.4 %while.66 = (s32[]{:T(128)}, bf16[512,512]{0,1:T(8,128)(2,1)}, f32[8,512,512]{1,2,0:T(8,128)}, bf16[8,2,512,512]{3,2,1,0:T(8,128)(2,1)}, f32[8,512,512]{1,2,0:T(8,128)}, /*index=5*/bf16[8,512,512]{2,1,0:T(8,128)(2,1)}, s32[]{:T(128)}) while((s32[]{:T(128)}, bf16[512,512]{0,1:T(8,128)(2,1)}, f32[8,512,512]{1,2,0:T(8,128)}, ...), condition=%wide.region_5.6_spmd, body=%wide.region_4.5_spmd.sunk | while | flops 806617088 | bytes 17302612 | solution.py:62
  303.0 4.3 broadcast.158
  307.4 67.7 %while.69 = (s32[]{:T(128)}, bf16[512,512]{0,1:T(8,128)(2,1)}, f32[8,512,512]{1,2,0:T(8,128)}, f32[8,512,512]{1,2,0:T(8,128)}, bf16[8,2,512,512]{3,2,1,0:T(8,128...) while((s32[]{:T(128)}, bf16[512,512]{0,1:T(8,128)(2,1)}, ...), condition=%wide.region_7.8_spmd.clone, body=%wide.region_6.7_spmd.clone.sunk | while | flops 807403520 | bytes 15204483 | solution.py:69
  375.0 9.9 %subtract_bitcast_fusion = (f32[1,8,512,256]{2,3,1,0:T(8,128)}, f32[1,8,512,256]{2,3,1,0:T(8,128)}) fusion(f32[8,512,512]{1,2,0:T(8,128)} %get-tuple-element.338, f32[]{:T(128)S(6)} %add.169, f32[]{:T(128)S(6)} %sub.71, f32[]{:T(128)} %bitcast.8, bf16[1,8,512,256]{2,3,1,0:T(8,128)(2,1)} %copy-done.2, f32[]{:T(128)} %bitcast.27), kind=kLoop, calls=%fused_computation.61 | loop fusion | flops 9437184 | bytes 18874384 | tf_op jit(solution)/shard_map/broadcast_in_dim | solution.py:110
  386.0 51.5 %reduce-scatter.3.cloned.1.call-done = f32[1,2,512,256]{2,3,1,0:T(8,128)} async-done(((f32[1,8,512,256]{2,3,1,0:T(8,128)}), f32[1,2,512,256]{2,3,1,0:T(8,128)}) %reduce-scatter.3.cloned.1.call-update) | async-done | bytes 1048592 | tf_op jit(solution)/shard_map/reduce_scatter | solution.py:109
  437.4 3.4 convolution_bitcast_fusion.6
  440.8 45.5 %reduce-scatter.5.cloned.1.call-done = f32[1,2,512,256]{2,3,1,0:T(8,128)} async-done(((f32[1,8,512,256]{2,3,1,0:T(8,128)}), f32[1,2,512,256]{2,3,1,0:T(8,128)}) %reduce-scatter.5.cloned.1.call-update) | async-done | bytes 1048592 | tf_op jit(solution)/shard_map/reduce_scatter | solution.py:110
  486.3 3.3 convolution_bitcast_fusion.5
  490.0 148.1 %all-reduce.5.cloned.1.call-done = (f32[256,256]{0,1:T(8,128)}, f32[256,256]{0,1:T(8,128)}) async-done(((f32[256,256]{0,1:T(8,128)}, f32[256,256]{0,1:T(8,128)}), (f32[256,256]{0,1:T(8,128)}, f32[256,256]{0,1:T(8,128)})) %all-reduce.5.cloned.1.call-update) | async-done | bytes 524304 | tf_op jit(solution)/shard_map/psum | solution.py:115
  640.3 11.7 %cholesky.50 = f32[128,128]{1,0:T(8,128)S(1)} custom-call(f32[128,128]{1,0:T(8,128)S(1)} %cholesky.118), custom_call_target="Cholesky" | custom-call | tf_op jit(solution)/shard_map/jit(cholesky)/cholesky | solution.py:119
  652.1 9.8 %custom-call.17 = f32[1,128,128]{1,2,0:T(8,128)S(1)} custom-call(f32[1,128,128]{2,1,0:T(8,128)S(1)} %get-tuple-element.519), custom_call_target="InvertDiagBlocksLowerTriangular" | custom-call | tf_op jit(solution)/shard_map/jit(cholesky)/cholesky | solution.py:119
  662.4 11.9 %cholesky.105 = f32[128,128]{1,0:T(8,128)S(1)} custom-call(f32[128,128]{1,0:T(8,128)S(1)} %convolution_subtract_fusion.3), custom_call_target="Cholesky" | custom-call | tf_op jit(solution)/shard_map/jit(cholesky)/cholesky | solution.py:119
  677.0 4.0 while.67
  681.0 19.7 %custom-call.18 = f32[2,128,128]{1,2,0:T(8,128)S(1)} custom-call(f32[2,128,128]{2,1,0:T(8,128)S(1)} %get-tuple-element.354), custom_call_target="InvertDiagBlocksLowerTriangular" | custom-call | tf_op jit(solution)/shard_map/triangular_solve | solution.py:17
  (252 shorter events, 309.3 us)
Async XLA Ops:
  7.2 430.3 %reduce-scatter.3.cloned.1.call-start = ((), (), s32[]{:S(2)}) async-start(), calls=%async_computation.2 | async-start | bytes 5242880 | tf_op jit(solution)/shard_map/reduce_scatter | solution.py:109
  15.4 6.9 copy-start.2
  15.9 2.1 copy-start
  18.0 4.2 copy-start.3
  168.3 28.2 %collective-permute-start = (f32[512,512]{0,1:T(8,128)S(1)}, f32[512,512]{0,1:T(8,128)S(1)}, u32[]{:S(2)}, u32[]{:S(2)}) collective-permute-start(f32[512,512]{0,1:T(8,128)S(1)} %slice_bitcast_fusion.1), channel_id=1, source_target_pairs={{1,0},{2,1},{3,2},{4,3},{5,4},{6,5},{7,6},{8,7},{9,8},{10,9},{11,1... | collective-permute-start | bytes 3145736 | tf_op jit(solution)/shard_map/ppermute | solution.py:13
  197.3 10.2 %copy-start.5 = (f32[1,4]{1,0:T(1,128)S(1)}, f32[1,4]{1,0:T(1,128)}, u32[]{:S(2)}) copy-start(f32[1,4]{1,0:T(1,128)} %param.23) | copy-start | bytes 52
  200.3 26.9 %collective-permute-start.1 = (f32[512,512]{0,1:T(8,128)}, f32[512,512]{0,1:T(8,128)}, u32[]{:S(2)}, u32[]{:S(2)}) collective-permute-start(f32[512,512]{0,1:T(8,128)} %convolution_bitcast_fusion.4), channel_id=1, source_target_pairs={{0,1},{1,2},{2,3},{3,4},{4,5},{5,6},{6,7},{7,8},{8,9},{9,10},{10,1... | collective-permute-start | bytes 3145736 | tf_op jit(solution)/shard_map/ppermute | solution.py:13
  212.9 14.2 %copy-start.1 = (f32[8,512,256]{1,2,0:T(8,128)S(1)}, f32[8,512,256]{1,2,0:T(8,128)}, u32[]{:S(2)}) copy-start(f32[8,512,256]{1,2,0:T(8,128)} %copy-done) | copy-start | bytes 12582916
  385.0 101.3 %reduce-scatter.5.cloned.1.call-start = ((), (), s32[]{:S(2)}) async-start(), calls=%async_computation.3 | async-start | bytes 5242880 | tf_op jit(solution)/shard_map/reduce_scatter | solution.py:110
  385.8 252.4 %all-reduce.5.cloned.1.call-start = ((), (), s32[]{:S(2)}) async-start(), calls=%async_computation.4 | async-start | bytes 1048576 | tf_op jit(solution)/shard_map/psum | solution.py:115
  437.4 52.2 %copy-start.4 = (f32[1,2,512,256]{2,3,1,0:T(8,128)S(1)}, f32[1,2,512,256]{2,3,1,0:T(8,128)}, u32[]{:S(2)}) copy-start(f32[1,2,512,256]{2,3,1,0:T(8,128)} %reduce-scatter.3.cloned.1.call-done) | copy-start | bytes 3145732
Sparse Core Ops, SparseCore 0:
  385.1 52.2 reduce-scatter.2
  440.0 46.3 reduce-scatter.4
  491.8 146.2 all-reduce.4
where the time goes:
time: 726 us; the launch traced here: 714 us
  waiting for transfers between devices  282 us (39%)
  other arithmetic  176 us (24%)
  local copies, waits for them, and re-layouts  127 us (17%)
  matrix products  99.8 us (14%)
  between operations  20.4 us (3%)
  starting transfers between devices  8.82 us (1%)
    psum x1, waiting for transfers between devices, on_device(): lax.psum((gram_part, projected_part), ('pole', 'dom'))  148 us
    dot_general x35, matrix products, complex_product(): jnp.dot(stacked, vectors.astype(jnp.bfloat16), preferred_element_type=jnp...  83.1 us
    dynamic_slice x64, local copies, waits for them, and re-layouts, partition_solve(): lax.scan(forward_step, initial, (inverse, source, previous))  82.9 us
    dynamic_update_slice x32, other arithmetic, partition_solve(): lax.scan(forward_step, initial, (inverse, source, previous))  60.9 us
    reduce_scatter x1, waiting for transfers between devices, on_device(): lax.psum_scatter(filtered_term[None], 'pole', scatter_dimension=1, tiled=...  51.5 us
    reduce_scatter x1, waiting for transfers between devices, on_device(): lax.psum_scatter(shifted_term[None], 'pole', scatter_dimension=1, tiled=T...  45.5 us
    ppermute x2, waiting for transfers between devices, shifted(): return lax.ppermute(x, axis, pairs)  36 us
    add x16, other arithmetic, backward_step(): partial_value + complex_product(block_inverse, real_product(couple_next,...  35.2 us
  transfers between devices with their start and end apart: 5, of which 5 were waited for; matrix products, arithmetic and copies ran while one was open for 1% of the time, Pallas kernels for 0%

commit v1 on v0

--- a/solution.py
+++ b/solution.py
@@ -112,7 +112,7 @@
     own_rows = owned[0].reshape(count * B, M)
     gram_part = inner_products(own_rows, own_rows)
     projected_part = inner_products(own_rows, shifted_owned[0].reshape(count * B, M))
-    gram_total, projected_total = lax.psum((gram_part, projected_part), ("pole", "dom"))
+    gram_total, projected_total = lax.psum(lax.psum((gram_part, projected_part), "dom"), "pole")
     row_total = blocks * B * lax.axis_size("dom")
     gram = gram_total / row_total
     projected = projected_total / row_total

time: 726 us -> 970 us (1.34)
  waiting for transfers between devices: 282 us -> 525 us
    psum x1 -> x2, waiting for transfers between devices: 148 us -> 392 us  [the longest x1 329 us: on_device(): lax.psum((gram_part, projected_part), 'dom')]
  transfers between devices with their start and end apart: 5 -> 6, of which waited for: 5 -> 6; matrix products, arithmetic and copies ran while one was open for 1% -> 1% of each run, Pallas kernels for 0% -> 0%
where the time goes in v1:
time: 970 us; the launch traced here: 958 us
  waiting for transfers between devices  525 us (54%)
  other arithmetic  176 us (18%)
  local copies, waits for them, and re-layouts  127 us (13%)
  matrix products  99.8 us (10%)
  between operations  20.6 us (2%)
    psum x1, waiting for transfers between devices, on_device(): lax.psum((gram_part, projected_part), 'dom')  329 us
    dot_general x35, matrix products, complex_product(): jnp.dot(stacked, vectors.astype(jnp.bfloat16), preferred_element_type=jnp...  83 us
    dynamic_slice x64, local copies, waits for them, and re-layouts, partition_solve(): lax.scan(forward_step, initial, (inverse, source, previous))  82.9 us
    psum x1, waiting for transfers between devices, on_device(): lax.psum(lax.psum((gram_part, projected_part), 'dom'), 'pole')  62.5 us
    dynamic_update_slice x32, other arithmetic, partition_solve(): lax.scan(forward_step, initial, (inverse, source, previous))  60.9 us
    reduce_scatter x1, waiting for transfers between devices, on_device(): lax.psum_scatter(filtered_term[None], 'pole', scatter_dimension=1, tiled=...  51.7 us
    reduce_scatter x1, waiting for transfers between devices, on_device(): lax.psum_scatter(shifted_term[None], 'pole', scatter_dimension=1, tiled=T...  45.5 us
    ppermute x2, waiting for transfers between devices, shifted(): return lax.ppermute(x, axis, pairs)  35.8 us
  transfers between devices with their start and end apart: 6, of which 6 were waited for; matrix products, arithmetic and copies ran while one was open for 1% of the time, Pallas kernels for 0%

profile of v1, /device:TPU:1, one launch (start us, length us, event | category | flops | bytes accessed | tf_op | source)
XLA Modules:
  0.0 958.2 jit_solution(1234657980538290111)
XLA Ops:
  7.2 4.2 slice_bitcast_fusion
  18.0 4.2 concatenate.76
  24.6 4.3 broadcast.158.clone.2
  29.8 65.2 %while.65 = (s32[]{:T(128)}, bf16[512,512]{0,1:T(8,128)(2,1)}, f32[8,512,512]{1,2,0:T(8,128)}, bf16[8,2,512,512]{3,2,1,0:T(8,128)(2,1)}, f32[8,512,512]{1,2,0:T(8,128)}, /*index=5*/bf16[8,512,512]{2,1,0:T(8,128)(2,1)}, s32[]{:T(128)}) while((s32[]{:T(128)}, bf16[512,512]{0,1:T(8,128)(2,1)}, f32[8,512,512]{1,2,0:T(8,128)}, ...), condition=%wide.region_1.2_spmd, body=%wide.region_0.1_spmd.sunk | while | flops 806617088 | bytes 17302612 | solution.py:62
  95.0 4.3 broadcast.158.clone.1
  99.3 67.8 %while.68 = (s32[]{:T(128)}, bf16[512,512]{0,1:T(8,128)(2,1)}, f32[8,512,512]{1,2,0:T(8,128)}, f32[8,512,512]{1,2,0:T(8,128)}, bf16[8,2,512,512]{3,2,1,0:T(8,128...) while((s32[]{:T(128)}, bf16[512,512]{0,1:T(8,128)(2,1)}, ...), condition=%wide.region_3.4_spmd.clone, body=%wide.region_2.3_spmd.clone.sunk | while | flops 807403520 | bytes 15204483 | solution.py:69
  174.0 22.7 %collective-permute-done = f32[512,512]{0,1:T(8,128)S(1)} collective-permute-done((f32[512,512]{0,1:T(8,128)S(1)}, f32[512,512]{0,1:T(8,128)S(1)}, u32[]{:S(2)}, u32[]{:S(2)}) %collective-permute-start) | collective-permute-done | bytes 1048608 | tf_op jit(solution)/shard_map/ppermute | solution.py:13
  200.4 7.2 collective-permute-start.1
  214.1 13.1 %collective-permute-done.1 = f32[512,512]{0,1:T(8,128)} collective-permute-done((f32[512,512]{0,1:T(8,128)}, f32[512,512]{0,1:T(8,128)}, u32[]{:S(2)}, u32[]{:S(2)}) %collective-permute-start.1) | collective-permute-done | bytes 1048608 | tf_op jit(solution)/shard_map/ppermute | solution.py:13
  232.5 4.3 broadcast.158.clone
  237.7 65.5 %while.66 = (s32[]{:T(128)}, bf16[512,512]{0,1:T(8,128)(2,1)}, f32[8,512,512]{1,2,0:T(8,128)}, bf16[8,2,512,512]{3,2,1,0:T(8,128)(2,1)}, f32[8,512,512]{1,2,0:T(8,128)}, /*index=5*/bf16[8,512,512]{2,1,0:T(8,128)(2,1)}, s32[]{:T(128)}) while((s32[]{:T(128)}, bf16[512,512]{0,1:T(8,128)(2,1)}, f32[8,512,512]{1,2,0:T(8,128)}, ...), condition=%wide.region_5.6_spmd, body=%wide.region_4.5_spmd.sunk | while | flops 806617088 | bytes 17302612 | solution.py:62
  303.2 4.3 broadcast.158
  307.5 67.7 %while.69 = (s32[]{:T(128)}, bf16[512,512]{0,1:T(8,128)(2,1)}, f32[8,512,512]{1,2,0:T(8,128)}, f32[8,512,512]{1,2,0:T(8,128)}, bf16[8,2,512,512]{3,2,1,0:T(8,128...) while((s32[]{:T(128)}, bf16[512,512]{0,1:T(8,128)(2,1)}, ...), condition=%wide.region_7.8_spmd.clone, body=%wide.region_6.7_spmd.clone.sunk | while | flops 807403520 | bytes 15204483 | solution.py:69
  375.3 10.0 %subtract_bitcast_fusion = (f32[1,8,512,256]{2,3,1,0:T(8,128)}, f32[1,8,512,256]{2,3,1,0:T(8,128)}) fusion(f32[8,512,512]{1,2,0:T(8,128)} %get-tuple-element.338, f32[]{:T(128)S(6)} %add.173, f32[]{:T(128)S(6)} %sub.71, f32[]{:T(128)} %bitcast.8, bf16[1,8,512,256]{2,3,1,0:T(8,128)(2,1)} %copy-done.2, f32[]{:T(128)} %bitcast.27), kind=kLoop, calls=%fused_computation.61 | loop fusion | flops 9437184 | bytes 18874384 | tf_op jit(solution)/shard_map/broadcast_in_dim | solution.py:110
  386.1 51.7 %reduce-scatter.3.cloned.1.call-done = f32[1,2,512,256]{2,3,1,0:T(8,128)} async-done(((f32[1,8,512,256]{2,3,1,0:T(8,128)}), f32[1,2,512,256]{2,3,1,0:T(8,128)}) %reduce-scatter.3.cloned.1.call-update) | async-done | bytes 1048592 | tf_op jit(solution)/shard_map/reduce_scatter | solution.py:109
  437.7 3.4 convolution_bitcast_fusion.6
  441.1 45.5 %reduce-scatter.5.cloned.1.call-done = f32[1,2,512,256]{2,3,1,0:T(8,128)} async-done(((f32[1,8,512,256]{2,3,1,0:T(8,128)}), f32[1,2,512,256]{2,3,1,0:T(8,128)}) %reduce-scatter.5.cloned.1.call-update) | async-done | bytes 1048592 | tf_op jit(solution)/shard_map/reduce_scatter | solution.py:110
  490.1 329.1 %all-reduce.7.cloned.1.call-done = (f32[256,256]{0,1:T(8,128)}, f32[256,256]{0,1:T(8,128)}) async-done(((f32[256,256]{0,1:T(8,128)}, f32[256,256]{0,1:T(8,128)}), (f32[256,256]{0,1:T(8,128)}, f32[256,256]{0,1:T(8,128)})) %all-reduce.7.cloned.1.call-update) | async-done | bytes 524304 | tf_op jit(solution)/shard_map/psum | solution.py:115
  819.6 62.5 %all-reduce.9.cloned.1.call-done = (f32[256,256]{0,1:T(8,128)}, f32[256,256]{0,1:T(8,128)}) async-done(((f32[256,256]{0,1:T(8,128)}, f32[256,256]{0,1:T(8,128)}), (f32[256,256]{0,1:T(8,128)}, f32[256,256]{0,1:T(8,128)})) %all-reduce.9.cloned.1.call-update) | async-done | bytes 524304 | tf_op jit(solution)/shard_map/psum | solution.py:115
  884.3 11.7 %cholesky.50 = f32[128,128]{1,0:T(8,128)S(1)} custom-call(f32[128,128]{1,0:T(8,128)S(1)} %cholesky.118), custom_call_target="Cholesky" | custom-call | tf_op jit(solution)/shard_map/jit(cholesky)/cholesky | solution.py:119
  896.1 9.8 %custom-call.17 = f32[1,128,128]{1,2,0:T(8,128)S(1)} custom-call(f32[1,128,128]{2,1,0:T(8,128)S(1)} %get-tuple-element.521), custom_call_target="InvertDiagBlocksLowerTriangular" | custom-call | tf_op jit(solution)/shard_map/jit(cholesky)/cholesky | solution.py:119
  906.4 11.7 %cholesky.105 = f32[128,128]{1,0:T(8,128)S(1)} custom-call(f32[128,128]{1,0:T(8,128)S(1)} %convolution_subtract_fusion.3), custom_call_target="Cholesky" | custom-call | tf_op jit(solution)/shard_map/jit(cholesky)/cholesky | solution.py:119
  920.8 4.2 while.67
  925.0 19.7 %custom-call.18 = f32[2,128,128]{1,2,0:T(8,128)S(1)} custom-call(f32[2,128,128]{2,1,0:T(8,128)S(1)} %get-tuple-element.354), custom_call_target="InvertDiagBlocksLowerTriangular" | custom-call | tf_op jit(solution)/shard_map/triangular_solve | solution.py:17
  (255 shorter events, 312.9 us)
Async XLA Ops:
  7.2 430.6 %reduce-scatter.3.cloned.1.call-start = ((), (), s32[]{:S(2)}) async-start(), calls=%async_computation.2 | async-start | bytes 5242880 | tf_op jit(solution)/shard_map/reduce_scatter | solution.py:109
  15.4 6.9 copy-start.2
  16.0 2.1 copy-start
  18.0 4.3 copy-start.3
  168.4 28.2 %collective-permute-start = (f32[512,512]{0,1:T(8,128)S(1)}, f32[512,512]{0,1:T(8,128)S(1)}, u32[]{:S(2)}, u32[]{:S(2)}) collective-permute-start(f32[512,512]{0,1:T(8,128)S(1)} %slice_bitcast_fusion.1), channel_id=1, source_target_pairs={{1,0},{2,1},{3,2},{4,3},{5,4},{6,5},{7,6},{8,7},{9,8},{10,9},{11,1... | collective-permute-start | bytes 3145736 | tf_op jit(solution)/shard_map/ppermute | solution.py:13
  197.4 10.2 %copy-start.5 = (f32[1,4]{1,0:T(1,128)S(1)}, f32[1,4]{1,0:T(1,128)}, u32[]{:S(2)}) copy-start(f32[1,4]{1,0:T(1,128)} %param.23) | copy-start | bytes 52
  200.4 26.9 %collective-permute-start.1 = (f32[512,512]{0,1:T(8,128)}, f32[512,512]{0,1:T(8,128)}, u32[]{:S(2)}, u32[]{:S(2)}) collective-permute-start(f32[512,512]{0,1:T(8,128)} %convolution_bitcast_fusion.4), channel_id=1, source_target_pairs={{0,1},{1,2},{2,3},{3,4},{4,5},{5,6},{6,7},{7,8},{8,9},{9,10},{10,1... | collective-permute-start | bytes 3145736 | tf_op jit(solution)/shard_map/ppermute | solution.py:13
  213.2 14.1 %copy-start.1 = (f32[8,512,256]{1,2,0:T(8,128)S(1)}, f32[8,512,256]{1,2,0:T(8,128)}, u32[]{:S(2)}) copy-start(f32[8,512,256]{1,2,0:T(8,128)} %copy-done) | copy-start | bytes 12582916
  385.3 101.4 %reduce-scatter.5.cloned.1.call-start = ((), (), s32[]{:S(2)}) async-start(), calls=%async_computation.3 | async-start | bytes 5242880 | tf_op jit(solution)/shard_map/reduce_scatter | solution.py:110
  386.0 433.2 %all-reduce.7.cloned.1.call-start = ((), (), s32[]{:S(2)}) async-start(), calls=%async_computation.4 | async-start | bytes 1048576 | tf_op jit(solution)/shard_map/psum | solution.py:115
  437.7 381.5 %copy-start.4 = (f32[1,2,512,256]{2,3,1,0:T(8,128)S(1)}, f32[1,2,512,256]{2,3,1,0:T(8,128)}, u32[]{:S(2)}) copy-start(f32[1,2,512,256]{2,3,1,0:T(8,128)} %reduce-scatter.3.cloned.1.call-done) | copy-start | bytes 3145732
  489.9 392.2 %all-reduce.9.cloned.1.call-start = ((), (), s32[]{:S(2)}) async-start(), calls=%async_computation.5 | async-start | bytes 1048576 | tf_op jit(solution)/shard_map/psum | solution.py:115
Sparse Core Ops, SparseCore 0:
  385.4 52.3 reduce-scatter.2
  440.3 46.3 reduce-scatter.4
  490.0 329.1 all-reduce.6
  821.8 60.3 all-reduce.8
